TPU v7x, 32 devices: a whole 2x2x4 slice. The times are simulated.
32 devices in a mesh: blk: 8 (over z, y), grp: 4 (over x, core).
Axes of the slice: x: 2, y: 2, z: 4, core: 2. Of those that a mesh axis runs over, the one named last changes fastest.
Arguments:
- queries: bfloat16 [4096, 4096], P(('blk', 'grp')), may hold values from -0.1875 to 0.1875
- passages: bfloat16 [64, 4096], P(('blk', 'grp')), may hold values from -5 to 5
- pool: bfloat16 [4096, 4096], P(('blk', 'grp')), may hold values from -5 to 5
- positive_ids: int32 [4096], P(('blk', 'grp')), may hold values from 0 to 15
- request_lists: int32 [32, 4, 32], P(('blk', 'grp')), may hold values from 0 to 127, as said below
- hard_refs: int32 [4096, 30], P(('blk', 'grp')), may hold values from 0 to 127, as said below
- hard_count: int32 [4096], P(('blk', 'grp')), may hold values from 1 to 30
Outputs:
- query_grad: bfloat16 [4096, 4096], P(('blk', 'grp'))
- query_loss: float32 [4096], P(('blk', 'grp'))
Inputs may be any that keep to these rules, and one draw needn't show every extreme that they name: `request_lists`: entries of one list are distinct rows of that owner's 128 pool rows. `hard_refs`: the first hard_count entries of a row are distinct; later entries are padding and unused.
All inputs are finite; a program needn't handle non-finite values.
Results may differ from a plain program's by a relative error of at most 0.0034.
Values may be sent and summed in bfloat16 or wider, within the bound.
A program may use at most 64 MiB of HBM per device.

v0:
```python
import jax
import jax.numpy as jnp
from jax import lax
from jax.sharding import PartitionSpec as P


def hard_mask(refs, count, span):
    table_iota = jnp.arange(span, dtype=jnp.int32)
    order = jnp.arange(refs.shape[1], dtype=jnp.int32)
    live = order[None, :] < count[:, None]
    hits = (refs[:, :, None] == table_iota[None, None, :]) & live[:, :, None]
    return jnp.sum(hits.astype(jnp.float32), axis=1)


def body(queries, passages, pool, positive_ids, request_lists, hard_refs, hard_count):
    owners = request_lists.shape[1]
    slot_count = request_lists.shape[2]
    gathered = lax.all_gather(pool, "grp", axis=0, tiled=True)
    pool_depth = pool.shape[0]
    owner_base = jnp.arange(owners, dtype=jnp.int32)[:, None] * pool_depth
    row_index = (owner_base + request_lists[0]).reshape(owners * slot_count)
    hard_table = gathered[row_index]
    hard_logits = jnp.dot(queries, hard_table.T, preferred_element_type=jnp.float32)
    present = hard_mask(hard_refs, hard_count, owners * slot_count)
    hard_peak = jnp.max(jnp.where(present > 0, hard_logits, -jnp.inf), axis=1)
    cycle_rows = lax.all_gather(passages, "blk", axis=0, tiled=True)
    cycle_logits = jnp.dot(queries, cycle_rows.T, preferred_element_type=jnp.float32)
    peak_value = jnp.maximum(hard_peak, jnp.max(cycle_logits, axis=1))
    cycle_exp = jnp.exp(cycle_logits - peak_value[:, None])
    hard_exp = present * jnp.exp(hard_logits - peak_value[:, None])
    denominator = jnp.sum(cycle_exp, axis=1) + jnp.sum(hard_exp, axis=1)
    cycle_iota = jnp.arange(cycle_rows.shape[0], dtype=jnp.int32)
    onehot = (cycle_iota[None, :] == positive_ids[:, None]).astype(jnp.float32)
    chosen = jnp.sum(cycle_logits * onehot, axis=1)
    cycle_weights = (cycle_exp / denominator[:, None] - onehot).astype(jnp.bfloat16)
    cycle_part = jnp.dot(cycle_weights, cycle_rows, preferred_element_type=jnp.float32)
    hard_weights = (hard_exp / denominator[:, None]).astype(jnp.bfloat16)
    gradient = cycle_part + jnp.dot(hard_weights, hard_table, preferred_element_type=jnp.float32)
    query_loss = jnp.log(denominator) + peak_value - chosen
    return (gradient.astype(jnp.bfloat16), query_loss)


def solution(mesh):
    return jax.shard_map(
        body,
        mesh=mesh,
        in_specs=(
            P(("blk", "grp"), None),
            P(("blk", "grp"), None),
            P(("blk", "grp"), None),
            P(("blk", "grp")),
            P(("blk", "grp"), None, None),
            P(("blk", "grp"), None),
            P(("blk", "grp")),
        ),
        out_specs=(P(("blk", "grp"), None), P(("blk", "grp"))),
        check_vma=False,
    )
```

profile of v0, /device:TPU:0, one launch (start us, length us, event | category | flops | bytes accessed | tf_op | source)
XLA Modules:
  0.0 61.7 jit_solution(39661543606083130)
XLA Ops:
  7.2 0.0 copy-start
  7.2 0.0 all-gather.3.cloned.1.call-start
  7.2 0.7 %all-gather.3.cloned.1.call-update = ((bf16[128,4096]{1,0:T(8,128)(2,1)}), bf16[512,4096]{1,0:T(8,128)(2,1)}) async-update(((), (), s32[]{:S(2)}) %all-gather.3.cloned.1.call-start, bf16[128,4096]{1,0:T(8,128)(2,1)} %param.9) | async-update | bytes 6291480
  7.9 0.8 %squeeze.3 = s32[128,1]{0,1:T(1,128)S(1)} reshape(s32[1,4,32]{2,1,0:T(4,128)} %param.11) | data formatting | bytes 1024 | tf_op jit(solution)/shard_map/squeeze | solution.py:21
  8.7 0.1 add.44
  8.8 0.1 add.45
  8.8 0.7 %iota_compare_fusion.1 = pred[128,30]{0,1:T(8,128)(4,1)S(1)} fusion(s32[128]{0:T(128)} %param.13), kind=kLoop, calls=%fused_computation.12 | loop fusion | flops 3840 | bytes 4352 | tf_op jit(solution)/shard_map/lt | solution.py:10
  9.5 3.1 %convert_reduce_fusion = f32[128,128]{1,0:T(8,128)S(1)} fusion(s32[128,30]{0,1:T(8,128)} %param.12, pred[128,30]{0,1:T(8,128)(4,1)S(1)} %iota_compare_fusion.1), kind=kLoop, calls=%fused_computation.3 | loop fusion | flops 1949696 | bytes 84736 | tf_op jit(solution)/shard_map/reduce_sum | solution.py:12
  12.7 0.1 copy.11
  12.8 32.5 %all-gather = bf16[8,2,4096]{2,1,0:T(2,128)(2,1)S(1)} all-gather(bf16[1,2,4096]{2,1,0:T(2,128)(2,1)} %bitcast.11), channel_id=1, replica_groups=mesh['blk'=8,'grp'=4] {'blk'}, dimensions={0}, use_global_device_ids=true | all-gather | bytes 147456 | tf_op jit(solution)/shard_map/all_gather | solution.py:26
  45.3 0.1 reshape.80
  45.4 0.0 copy-done
  45.4 0.4 fusion.10
  45.8 1.0 %all-gather.3.cloned.1.call-done = bf16[512,4096]{1,0:T(8,128)(2,1)} async-done(((bf16[128,4096]{1,0:T(8,128)(2,1)}), bf16[512,4096]{1,0:T(8,128)(2,1)}) %all-gather.3.cloned.1.call-update) | async-done | bytes 4194320 | tf_op jit(solution)/shard_map/all_gather | solution.py:18
  46.8 4.9 %gather_fusion = bf16[128,4096]{1,0:T(8,128)(2,1)S(1)} fusion(bf16[512,4096]{1,0:T(8,128)(2,1)} %all-gather.3.cloned.1.call-done, s32[1024]{0:T(1024)S(1)} %pad_clamp_fusion), kind=kCustom, calls=%fused_computation | custom fusion | bytes 2097664 | tf_op jit(solution)/shard_map/gather | solution.py:22
  51.7 0.0 copy-start.1
  51.7 0.5 select_reduce_fusion
  52.2 0.1 copy-done.1
  52.4 0.5 add_subtract_fusion
  52.9 0.5 fusion.5
  53.4 1.5 %fusion = bf16[128,4096]{1,0:T(8,128)(2,1)} fusion(f32[128,4096]{1,0:T(8,128)S(1)} %fusion.5, bf16[128,4096]{1,0:T(8,128)(2,1)S(1)} %gather_fusion, f32[128]{0:T(128)S(1)} %get-tuple-element.5, f32[128,128]{0,1:T(8,128)S(1)} %copy.11, f32[128,128]{0,1:T(8,128)S(1)} %get-tuple-element.7, f32[128]{0:T(128)S(1)} %max.7), kind=kOutput, calls=%fused_computation.2 | convolution fusion | flops 135331840 | bytes 4326400 | tf_op jit(solution)/shard_map/dot_general | solution.py:38
  (6 shorter events, 0.1 us)
Async XLA Ops:
  7.2 38.2 %copy-start = (bf16[128,4096]{1,0:T(8,128)(2,1)S(1)}, bf16[128,4096]{1,0:T(8,128)(2,1)}, u32[]{:S(2)}) copy-start(bf16[128,4096]{1,0:T(8,128)(2,1)} %param.7) | copy-start | bytes 3145732
  7.2 39.6 %all-gather.3.cloned.1.call-start = ((), (), s32[]{:S(2)}) async-start(), calls=%async_computation | async-start | bytes 5242880 | tf_op jit(solution)/shard_map/all_gather | solution.py:18
  51.7 0.7 %copy-start.1 = (s32[128]{0:T(128)S(1)}, s32[128]{0:T(128)}, u32[]{:S(2)}) copy-start(s32[128]{0:T(128)} %param.10) | copy-start | bytes 1540
Sparse Core Ops, SparseCore 0:
  9.6 37.1 all-gather.2
where the time goes:
time: 62.1 us; the launch traced here: 61.7 us
  blocking collectives  32.5 us (52%)
  between operations  14.1 us (23%)
  local copies, waits for them, and re-layouts  6.15 us (10%)
  other arithmetic  4.43 us (7%)
  matrix products  2.77 us (4%)
  waiting for transfers between devices  1.71 us (3%)
    all_gather x1, blocking collectives, body(): cycle_rows = lax.all_gather(passages, 'blk', axis=0, tiled=True)  32.5 us
    gather x1, local copies, waits for them, and re-layouts, body(): hard_table = gathered[row_index]  4.93 us
    reduce_sum x1, other arithmetic, hard_mask(): return jnp.sum(hits.astype(jnp.float32), axis=1)  3.15 us
    dot_general x1, matrix products, body(): jnp.dot(hard_weights, hard_table, preferred_element_type=jnp.float32)  1.46 us
  transfers between devices with their start and end apart: 1, of which 1 were waited for; matrix products, arithmetic and copies ran while one was open for 9% of the time, Pallas kernels for 0%

commit v1 on v0

v1 whole, which is shorter than its diff:
```python
import functools

import jax
import jax.numpy as jnp
from jax import lax
from jax.experimental import pallas as pl
from jax.experimental.pallas import tpu as pltpu
from jax.sharding import PartitionSpec as P

MESH = pl.DeviceIdType.MESH
CHUNKS = 4
GRAD_TILES = 4
VMEM_LIMIT = 32 * 2**20
TILE_ROWS = 16


def iota(shape, axis):
    return lax.broadcasted_iota(jnp.int32, shape, axis)


def dot_nt(a, b):
    return lax.dot_general(a, b, (((1,), (1,)), ((), ())), preferred_element_type=jnp.float32)


def dot_nn(a, b):
    return jnp.dot(a, b, preferred_element_type=jnp.float32)


def kernel(n_blk, queries, passages, pool, positive, lists, refs, count, table, weights, loss,
           q_v, pass_v, pool_v, pos_v, list_v, refs_v, count_v,
           hot_out, hot_in, picked, packed,
           load_sem, hot_send, hot_recv, row_send, row_recv, pass_send, pass_recv):
    blk = lax.axis_index("blk")
    grp = lax.axis_index("grp")
    q_rows, depth = q_v.shape
    p_dev = pass_v.shape[0]
    pool_rows = pool_v.shape[0]
    owners, slots = list_v.shape
    span = owners * slots
    cycle = n_blk * p_dev
    folds = TILE_ROWS // p_dev
    fold_w = depth // folds
    width = depth // CHUNKS

    half, core = lax.div(grp, 2), lax.rem(grp, 2)
    far, side = 1 - half, 1 - core
    peers = {1: half * 2 + side, 2: far * 2 + core, 3: far * 2 + side}

    barrier = pltpu.get_barrier_semaphore()
    for step in (1, 2, 3):
        pl.semaphore_signal(barrier, inc=1, device_id={"grp": peers[step]}, device_id_type=MESH)

    def greet(step, carry):
        pl.semaphore_signal(barrier, inc=1, device_id={"blk": lax.rem(blk + step, n_blk)}, device_id_type=MESH)
        return carry

    lax.fori_loop(1, n_blk, greet, 0)

    loads = [
        pltpu.make_async_copy(src, dst, load_sem.at[i])
        for i, (src, dst) in enumerate((
            (lists, list_v), (passages, pass_v), (pool, pool_v), (refs, refs_v),
            (count, count_v), (positive, pos_v), (queries, q_v)))
    ]
    for load in loads:
        load.start()

    loads[0].wait()
    eye = iota((slots, slots), 0) == iota((slots, slots), 1)
    pool_iota = iota((slots, pool_rows), 1).astype(jnp.float32)
    wanted = list_v[...].astype(jnp.float32)
    for o in range(owners):
        column = jnp.sum(jnp.where(eye, wanted[o:o + 1, :], 0.0), axis=1, keepdims=True)
        hot_out[o * slots:(o + 1) * slots, :] = (pool_iota == column).astype(jnp.float32).astype(jnp.bfloat16)

    loads[1].wait()
    own = pass_v[...].astype(jnp.float32)
    fold_iota = iota((TILE_ROWS, fold_w), 0)
    folded = jnp.zeros((TILE_ROWS, fold_w), jnp.float32)
    for c in range(folds):
        for j in range(p_dev):
            folded = jnp.where(fold_iota == c * p_dev + j, own[j:j + 1, c * fold_w:(c + 1) * fold_w], folded)
    own_slot = pl.ds(pl.multiple_of(blk * TILE_ROWS, TILE_ROWS), TILE_ROWS)
    packed[own_slot, :] = folded.astype(jnp.bfloat16)

    pl.semaphore_wait(barrier, owners - 1 + n_blk - 1)

    hot_copies = {}
    for step in (2, 3, 1):
        hot_copies[step] = pltpu.make_async_remote_copy(
            src_ref=hot_out.at[pl.ds(pl.multiple_of(peers[step] * slots, slots), slots)],
            dst_ref=hot_in.at[pl.ds(step * slots, slots)],
            send_sem=hot_send.at[step], recv_sem=hot_recv.at[step],
            device_id={"grp": peers[step]}, device_id_type=MESH)
        hot_copies[step].start()

    def pass_copy(step):
        return pltpu.make_async_remote_copy(
            src_ref=packed.at[own_slot], dst_ref=packed.at[own_slot],
            send_sem=pass_send.at[step], recv_sem=pass_recv.at[step],
            device_id={"blk": lax.rem(blk + step, n_blk)}, device_id_type=MESH)

    def send_pass(step, carry):
        pass_copy(step).start()
        return carry

    lax.fori_loop(1, n_blk, send_pass, 0)

    own_rows = pl.ds(pl.multiple_of(grp * slots, slots), slots)
    hot_in[0:slots, :] = hot_out[own_rows, :]
    loads[2].wait()
    for step in (1, 2, 3):
        hot_copies[step].wait_recv()
    row_copies = []
    for c in range(CHUNKS):
        cols = slice(c * width, (c + 1) * width)
        rows = dot_nn(hot_in[...], pool_v[:, cols]).astype(jnp.bfloat16)
        picked[:, cols] = rows
        table[own_rows, cols] = rows[0:slots, :]
        sent = {}
        for step in (2, 3, 1):
            sent[step] = pltpu.make_async_remote_copy(
                src_ref=picked.at[pl.ds(step * slots, slots), pl.ds(c * width, width)],
                dst_ref=table.at[own_rows, pl.ds(c * width, width)],
                send_sem=row_send.at[step, c], recv_sem=row_recv.at[step, c],
                device_id={"grp": peers[step]}, device_id_type=MESH)
            sent[step].start()
        row_copies.append(sent)

    for load in loads[3:]:
        load.wait()
    hn = refs_v.shape[0]
    refs_t = jnp.where(iota((hn, q_rows), 0) < count_v[...], refs_v[...], -1)
    row_iota = iota((span, q_rows), 0)
    present = jnp.zeros((span, q_rows), jnp.float32)
    for i in range(hn):
        present = present + (row_iota == refs_t[i:i + 1, :]).astype(jnp.float32)

    def recv_pass(step, carry):
        pass_copy(step).wait()
        return carry

    lax.fori_loop(1, n_blk, recv_pass, 0)
    group_rows = folds * TILE_ROWS
    out_row, in_row = iota((group_rows, group_rows), 0), iota((group_rows, group_rows), 1)
    k = lax.rem(out_row, TILE_ROWS)
    source = lax.div(k, p_dev) * TILE_ROWS + lax.div(out_row, TILE_ROWS) * p_dev + lax.rem(k, p_dev)
    unfold = (source == in_row).astype(jnp.float32).astype(jnp.bfloat16)

    def unfold_group(i, carry):
        block = packed[pl.ds(pl.multiple_of(i * group_rows, group_rows), group_rows), :]
        rows = dot_nn(unfold, block).astype(jnp.bfloat16)
        place = pl.ds(pl.multiple_of(span + i * TILE_ROWS, TILE_ROWS), TILE_ROWS)
        for c in range(folds):
            table[place, c * fold_w:(c + 1) * fold_w] = rows[c * TILE_ROWS:(c + 1) * TILE_ROWS, :]
        return carry

    lax.fori_loop(0, n_blk // folds, unfold_group, 0)
    cycle_logits = jnp.zeros((cycle, q_rows), jnp.float32)
    for c in range(CHUNKS):
        cols = slice(c * width, (c + 1) * width)
        cycle_logits = cycle_logits + dot_nt(table[span:span + cycle, cols], q_v[:, cols])
    cycle_peak = jnp.max(cycle_logits, axis=0, keepdims=True)
    onehot = (iota((cycle, q_rows), 0) == pos_v[...]).astype(jnp.float32)
    chosen = jnp.sum(cycle_logits * onehot, axis=0, keepdims=True)

    hard_logits = jnp.zeros((span, q_rows), jnp.float32)
    for c in range(CHUNKS):
        cols = slice(c * width, (c + 1) * width)
        for step in (1, 2, 3):
            row_copies[c][step].wait_recv()
        hard_logits = hard_logits + dot_nt(table[0:span, cols], q_v[:, cols])

    used = present > 0
    masked = jnp.where(used, hard_logits, -jnp.inf)
    peak = jnp.maximum(cycle_peak, jnp.max(masked, axis=0, keepdims=True))
    cycle_exp = jnp.exp(cycle_logits - peak)
    hard_exp = present * jnp.exp(jnp.where(used, hard_logits - peak, 0.0))
    denominator = jnp.sum(cycle_exp, axis=0, keepdims=True) + jnp.sum(hard_exp, axis=0, keepdims=True)
    loss[...] = jnp.log(denominator) + peak - chosen
    scale = 1.0 / denominator
    weights[:, 0:span] = (hard_exp * scale).T.astype(jnp.bfloat16)
    weights[:, span:span + cycle] = (cycle_exp * scale - onehot).T.astype(jnp.bfloat16)

    for step in (1, 2, 3):
        hot_copies[step].wait_send()
        for c in range(CHUNKS):
            row_copies[c][step].wait_send()


def grad_kernel(table, weights, loss, grad, loss_out, grad_v, sems):
    tiles = sems.shape[0] - 1
    width = grad_v.shape[1] // tiles
    copies = [pltpu.make_async_copy(loss, loss_out, sems.at[tiles])]
    copies[0].start()
    for c in range(tiles):
        cols = slice(c * width, (c + 1) * width)
        grad_v[:, cols] = dot_nn(weights[...], table[:, cols]).astype(jnp.bfloat16)
        here = pl.ds(c * width, width)
        copies.append(pltpu.make_async_copy(grad_v.at[:, here], grad.at[:, here], sems.at[c]))
        copies[-1].start()
    for copy in copies:
        copy.wait()


def body(n_blk, queries, passages, pool, positive_ids, request_lists, hard_refs, hard_count):
    q_rows, depth = queries.shape
    p_dev = passages.shape[0]
    pool_rows = pool.shape[0]
    _, owners, slots = request_lists.shape
    hn = hard_refs.shape[1]
    span, cycle = owners * slots, n_blk * p_dev
    bf16, f32, i32 = jnp.bfloat16, jnp.float32, jnp.int32
    dma = pltpu.SemaphoreType.DMA
    flops = 2 * depth * (2 * q_rows * (span + cycle) + span * pool_rows)
    in_vmem = pl.BlockSpec(memory_space=pltpu.VMEM)
    in_hbm = pl.BlockSpec(memory_space=pltpu.HBM)
    table, weights, loss = pl.pallas_call(
        functools.partial(kernel, n_blk),
        out_shape=(
            pltpu.VMEM((span + cycle, depth), bf16),
            pltpu.VMEM((q_rows, span + cycle), bf16),
            pltpu.VMEM((1, q_rows), f32),
        ),
        in_specs=[in_hbm] * 7,
        out_specs=(in_vmem,) * 3,
        scratch_shapes=[
            pltpu.VMEM((q_rows, depth), bf16),
            pltpu.VMEM((p_dev, depth), bf16),
            pltpu.VMEM((pool_rows, depth), bf16),
            pltpu.VMEM((1, q_rows), i32),
            pltpu.VMEM((owners, slots), i32),
            pltpu.VMEM((hn, q_rows), i32),
            pltpu.VMEM((1, q_rows), i32),
            pltpu.VMEM((span, pool_rows), bf16),
            pltpu.VMEM((span, pool_rows), bf16),
            pltpu.VMEM((span, depth), bf16),
            pltpu.VMEM((n_blk * TILE_ROWS, depth * p_dev // TILE_ROWS), bf16),
            dma((7,)), dma((4,)), dma((4,)), dma((4, CHUNKS)), dma((4, CHUNKS)),
            dma((n_blk,)), dma((n_blk,)),
        ],
        compiler_params=pltpu.CompilerParams(
            collective_id=0, has_side_effects=True, vmem_limit_bytes=VMEM_LIMIT),
        cost_estimate=pl.CostEstimate(
            flops=flops, bytes_accessed=4 * q_rows * depth, transcendentals=q_rows * (span + cycle)),
    )(*(pltpu.with_memory_space_constraint(x, pltpu.HBM) for x in (
        queries, passages, pool, positive_ids.reshape(1, q_rows), request_lists.reshape(owners, slots),
        hard_refs.T, hard_count.reshape(1, q_rows))))
    grad, loss = pl.pallas_call(
        grad_kernel,
        out_shape=(pltpu.HBM((q_rows, depth), bf16), pltpu.HBM((1, q_rows), f32)),
        in_specs=[in_vmem] * 3,
        out_specs=(in_hbm,) * 2,
        scratch_shapes=[pltpu.VMEM((q_rows, depth), bf16), dma((GRAD_TILES + 1,))],
        compiler_params=pltpu.CompilerParams(vmem_limit_bytes=VMEM_LIMIT),
        cost_estimate=pl.CostEstimate(
            flops=2 * depth * q_rows * (span + cycle), bytes_accessed=2 * q_rows * depth, transcendentals=0),
    )(table, weights, loss)
    return grad, loss.reshape(q_rows)


def solution(mesh):
    rows = P(("blk", "grp"), None)
    return jax.shard_map(
        functools.partial(body, mesh.shape["blk"]),
        mesh=mesh,
        in_specs=(rows, rows, rows, P(("blk", "grp")), P(("blk", "grp"), None, None), rows, P(("blk", "grp"))),
        out_specs=(rows, P(("blk", "grp"))),
        check_vma=False,
    )
```

time: 62.1 us -> 24.9 us (0.40)
  blocking collectives: 32.5 us -> 0 us
  Pallas kernels: 0 us -> 24 us
  between operations: 14.1 us -> 0.64 us
  local copies, waits for them, and re-layouts: 6.15 us -> 0 us
  other arithmetic: 4.43 us -> 0 us
  matrix products: 2.77 us -> 0 us
  waiting for transfers between devices: 1.71 us -> 0 us
    all_gather x1 -> x0, blocking collectives: 32.5 us -> none  [body(): cycle_rows = lax.all_gather(passages, 'blk', axis=0, tiled=True)]
    pallas_call x0 -> x2, Pallas kernels: none -> 24 us  [the longest x1 22.8 us: body(): pl.pallas_call(functools.partial(kernel, n_blk), out_shape=(pltpu.VMEM((s...]
    gather x1 -> x0, local copies, waits for them, and re-layouts: 4.93 us -> none  [body(): hard_table = gathered[row_index]]
    reduce_sum x3 -> x0, other arithmetic: 3.22 us -> none  [the longest x1 3.15 us: hard_mask(): return jnp.sum(hits.astype(jnp.float32), axis=1)]
    dot_general x4 -> x0, matrix products: 2.77 us -> none  [the longest x1 1.46 us: body(): jnp.dot(hard_weights, hard_table, preferred_element_type=jnp.float32)]
    all_gather x1 -> x0, waiting for transfers between devices: 1.03 us -> none  [body(): gathered = lax.all_gather(pool, 'grp', axis=0, tiled=True)]
    squeeze x1 -> x0, local copies, waits for them, and re-layouts: 0.76 us -> none  [body(): row_index = (owner_base + request_lists[0]).reshape(owners * slot_count)]
    unnamed x1 -> x0, waiting for transfers between devices: 0.68 us -> none
  transfers between devices with their start and end apart: 1 -> 0, of which waited for: 1 -> 0; matrix products, arithmetic and copies ran while one was open for 9% -> 0% of each run, Pallas kernels for 0% -> 0%
where the time goes in v1:
time: 24.9 us; the launch traced here: 24.7 us
  Pallas kernels  24 us (96%)
  between operations  0.64 us (3%)
    pallas_call x1, Pallas kernels, body(): pl.pallas_call(functools.partial(kernel, n_blk), out_shape=(pltpu.VMEM((s...  22.8 us
    pallas_call x1, Pallas kernels, body(): pl.pallas_call(grad_kernel, out_shape=(pltpu.HBM((q_rows, depth), bf16),...  1.23 us

profile of v1, /device:TPU:0, one launch (start us, length us, event | category | flops | bytes accessed | tf_op | source)
XLA Modules:
  0.0 24.7 jit_solution(14397305047038709702)
XLA Ops:
  0.6 22.8 %shard_map.86 = (bf16[144,4096]{1,0:T(8,128)(2,1)S(1)}, bf16[128,144]{1,0:T(8,128)(2,1)S(1)}, f32[1,128]{1,0:T(1,128)S(1)}) custom-call(bf16[128,4096]{1,0:T(8,128)(2,1)} %queries.1, bf16[2,4096]{1,0:T(2,128)(2,1)} %passages.1, bf16[128,4096]{1,0:T(8,128)(2,1)} %pool.1, s32[1,128]{1,0:T(1,128)} %bitcast.7, s32[4,32]{1,0:T(4,128)} %bitcast.6, ...), custom_call_target="tpu_custom_call" | custom-call | flops 436207616 | bytes 2097152 | tf_op jit(solution)/shard_map/pallas_call | solution.py:218
  23.5 1.2 %shard_map.87 = (bf16[128,4096]{1,0:T(8,128)(2,1)}, f32[1,128]{1,0:T(1,128)}) custom-call(bf16[144,4096]{1,0:T(8,128)(2,1)S(1)} %get-tuple-element.7.table, bf16[128,144]{1,0:T(8,128)(2,1)S(1)} %get-tuple-element.8.weights, f32[1,128]{1,0:T(1,128)S(1)} %get-tuple-element.9.loss), custom_call_target="tpu_custom_call" | custom-call | flops 150994944 | bytes 1048576 | tf_op jit(solution)/shard_map/pallas_call | solution.py:249

commit v2 on v1

--- a/solution.py
+++ b/solution.py
@@ -8,10 +8,9 @@
 from jax.sharding import PartitionSpec as P
 
 MESH = pl.DeviceIdType.MESH
-CHUNKS = 4
-GRAD_TILES = 4
 VMEM_LIMIT = 32 * 2**20
 TILE_ROWS = 16
+CHUNKS = 4
 
 
 def iota(shape, axis):
@@ -29,7 +28,7 @@
 def kernel(n_blk, queries, passages, pool, positive, lists, refs, count, table, weights, loss,
            q_v, pass_v, pool_v, pos_v, list_v, refs_v, count_v,
            hot_out, hot_in, picked, packed,
-           load_sem, hot_send, hot_recv, row_send, row_recv, pass_send, pass_recv):
+           load_sem, hot_send, hot_recv, row_send, row_recv, pass_send, pass_recv, go_sem):
     blk = lax.axis_index("blk")
     grp = lax.axis_index("grp")
     q_rows, depth = q_v.shape
@@ -43,18 +42,15 @@
     width = depth // CHUNKS
 
     half, core = lax.div(grp, 2), lax.rem(grp, 2)
-    far, side = 1 - half, 1 - core
-    peers = {1: half * 2 + side, 2: far * 2 + core, 3: far * 2 + side}
+    near, far_odd, far_even = half * 2 + 1 - core, (1 - half) * 2 + 1, (1 - half) * 2
+    peers = (far_odd, far_even, near)
+    is_hub = grp == 0
 
     barrier = pltpu.get_barrier_semaphore()
-    for step in (1, 2, 3):
-        pl.semaphore_signal(barrier, inc=1, device_id={"grp": peers[step]}, device_id_type=MESH)
-
-    def greet(step, carry):
-        pl.semaphore_signal(barrier, inc=1, device_id={"blk": lax.rem(blk + step, n_blk)}, device_id_type=MESH)
-        return carry
-
-    lax.fori_loop(1, n_blk, greet, 0)
+    for peer in peers:
+        @pl.when(peer != 0)
+        def _():
+            pl.semaphore_signal(barrier, inc=1, device_id={"grp": peer}, device_id_type=MESH)
 
     loads = [
         pltpu.make_async_copy(src, dst, load_sem.at[i])
@@ -72,6 +68,73 @@
     for o in range(owners):
         column = jnp.sum(jnp.where(eye, wanted[o:o + 1, :], 0.0), axis=1, keepdims=True)
         hot_out[o * slots:(o + 1) * slots, :] = (pool_iota == column).astype(jnp.float32).astype(jnp.bfloat16)
+
+    def slot_rows(owner):
+        return pl.ds(pl.multiple_of(owner * slots, slots), slots)
+
+    def hot_copy(source, target, peer):
+        return pltpu.make_async_remote_copy(
+            src_ref=hot_out.at[slot_rows(target)], dst_ref=hot_in.at[slot_rows(source)],
+            send_sem=hot_send.at[target], recv_sem=hot_recv.at[source],
+            device_id={"grp": peer}, device_id_type=MESH)
+
+    def row_copy(source, target, c, peer):
+        return pltpu.make_async_remote_copy(
+            src_ref=picked.at[c, slot_rows(target)], dst_ref=table.at[c, slot_rows(source)],
+            send_sem=row_send.at[target, c], recv_sem=row_recv.at[source, c],
+            device_id={"grp": peer}, device_id_type=MESH)
+
+    def pass_copy(step):
+        return pltpu.make_async_remote_copy(
+            src_ref=packed.at[own_slot], dst_ref=packed.at[own_slot],
+            send_sem=pass_send.at[step], recv_sem=pass_recv.at[step],
+            device_id={"blk": lax.rem(blk + step, n_blk)}, device_id_type=MESH)
+
+    @pl.when(jnp.logical_not(is_hub))
+    def _():
+        pl.semaphore_wait(barrier, owners - 1)
+        for peer in peers:
+            hot_copy(grp, peer, peer).start()
+
+    @pl.when(is_hub)
+    def _():
+        for peer in peers:
+            hot_copy(peer, grp, peer).wait_recv()
+        for peer in peers:
+            hot_copy(grp, peer, peer).start()
+
+        def greet(step, carry):
+            pl.semaphore_signal(
+                barrier, inc=1, device_id={"blk": lax.rem(blk + step, n_blk)}, device_id_type=MESH)
+            return carry
+
+        lax.fori_loop(1, n_blk, greet, 0)
+
+    hot_in[slot_rows(grp), :] = hot_out[slot_rows(grp), :]
+
+    def send_rows(c, first, last):
+        rows = dot_nn(hot_in[first * slots:last * slots, :], pool_v[:, c * width:(c + 1) * width])
+        picked[c, first * slots:last * slots, :] = rows.astype(jnp.bfloat16)
+        for peer in reversed(range(first, last)):
+            @pl.when(grp != peer)
+            def _():
+                row_copy(grp, peer, c, peer).start()
+
+    def hot_arrived(peer):
+        @pl.when(jnp.logical_and(jnp.logical_not(is_hub), grp != peer))
+        def _():
+            hot_copy(peer, grp, peer).wait_recv()
+
+    loads[2].wait()
+    for peer in range(1, owners):
+        hot_arrived(peer)
+    send_rows(0, 1, owners)
+    send_rows(1, 1, owners)
+    hot_arrived(0)
+    for c in range(CHUNKS):
+        send_rows(c, 0, 1)
+        if c + 2 < CHUNKS:
+            send_rows(c + 2, 1, owners)
 
     loads[1].wait()
     own = pass_v[...].astype(jnp.float32)
@@ -83,22 +146,15 @@
     own_slot = pl.ds(pl.multiple_of(blk * TILE_ROWS, TILE_ROWS), TILE_ROWS)
     packed[own_slot, :] = folded.astype(jnp.bfloat16)
 
-    pl.semaphore_wait(barrier, owners - 1 + n_blk - 1)
-
-    hot_copies = {}
-    for step in (2, 3, 1):
-        hot_copies[step] = pltpu.make_async_remote_copy(
-            src_ref=hot_out.at[pl.ds(pl.multiple_of(peers[step] * slots, slots), slots)],
-            dst_ref=hot_in.at[pl.ds(step * slots, slots)],
-            send_sem=hot_send.at[step], recv_sem=hot_recv.at[step],
-            device_id={"grp": peers[step]}, device_id_type=MESH)
-        hot_copies[step].start()
-
-    def pass_copy(step):
-        return pltpu.make_async_remote_copy(
-            src_ref=packed.at[own_slot], dst_ref=packed.at[own_slot],
-            send_sem=pass_send.at[step], recv_sem=pass_recv.at[step],
-            device_id={"blk": lax.rem(blk + step, n_blk)}, device_id_type=MESH)
+    @pl.when(is_hub)
+    def _():
+        pl.semaphore_wait(barrier, n_blk - 1)
+        for peer in peers:
+            pl.semaphore_signal(go_sem, inc=1, device_id={"grp": peer}, device_id_type=MESH)
+
+    @pl.when(jnp.logical_not(is_hub))
+    def _():
+        pl.semaphore_wait(go_sem, 1)
 
     def send_pass(step, carry):
         pass_copy(step).start()
@@ -106,26 +162,7 @@
 
     lax.fori_loop(1, n_blk, send_pass, 0)
 
-    own_rows = pl.ds(pl.multiple_of(grp * slots, slots), slots)
-    hot_in[0:slots, :] = hot_out[own_rows, :]
-    loads[2].wait()
-    for step in (1, 2, 3):
-        hot_copies[step].wait_recv()
-    row_copies = []
-    for c in range(CHUNKS):
-        cols = slice(c * width, (c + 1) * width)
-        rows = dot_nn(hot_in[...], pool_v[:, cols]).astype(jnp.bfloat16)
-        picked[:, cols] = rows
-        table[own_rows, cols] = rows[0:slots, :]
-        sent = {}
-        for step in (2, 3, 1):
-            sent[step] = pltpu.make_async_remote_copy(
-                src_ref=picked.at[pl.ds(step * slots, slots), pl.ds(c * width, width)],
-                dst_ref=table.at[own_rows, pl.ds(c * width, width)],
-                send_sem=row_send.at[step, c], recv_sem=row_recv.at[step, c],
-                device_id={"grp": peers[step]}, device_id_type=MESH)
-            sent[step].start()
-        row_copies.append(sent)
+    table[:, slot_rows(grp), :] = picked[:, slot_rows(grp), :]
 
     for load in loads[3:]:
         load.wait()
@@ -136,6 +173,16 @@
     for i in range(hn):
         present = present + (row_iota == refs_t[i:i + 1, :]).astype(jnp.float32)
 
+    def hard_part(c):
+        cols = slice(c * width, (c + 1) * width)
+        for peer in peers:
+            row_copy(peer, grp, c, peer).wait_recv()
+        return dot_nt(table[c, 0:span, :], q_v[:, cols])
+
+    hard_logits = hard_part(0)
+    for c in range(1, CHUNKS - 1):
+        hard_logits = hard_logits + hard_part(c)
+
     def recv_pass(step, carry):
         pass_copy(step).wait()
         return carry
@@ -152,24 +199,20 @@
         rows = dot_nn(unfold, block).astype(jnp.bfloat16)
         place = pl.ds(pl.multiple_of(span + i * TILE_ROWS, TILE_ROWS), TILE_ROWS)
         for c in range(folds):
-            table[place, c * fold_w:(c + 1) * fold_w] = rows[c * TILE_ROWS:(c + 1) * TILE_ROWS, :]
+            at, within = divmod(c * fold_w, width)
+            table[at, place, within:within + fold_w] = rows[c * TILE_ROWS:(c + 1) * TILE_ROWS, :]
         return carry
 
     lax.fori_loop(0, n_blk // folds, unfold_group, 0)
     cycle_logits = jnp.zeros((cycle, q_rows), jnp.float32)
     for c in range(CHUNKS):
         cols = slice(c * width, (c + 1) * width)
-        cycle_logits = cycle_logits + dot_nt(table[span:span + cycle, cols], q_v[:, cols])
+        cycle_logits = cycle_logits + dot_nt(table[c, span:span + cycle, :], q_v[:, cols])
     cycle_peak = jnp.max(cycle_logits, axis=0, keepdims=True)
     onehot = (iota((cycle, q_rows), 0) == pos_v[...]).astype(jnp.float32)
     chosen = jnp.sum(cycle_logits * onehot, axis=0, keepdims=True)
 
-    hard_logits = jnp.zeros((span, q_rows), jnp.float32)
-    for c in range(CHUNKS):
-        cols = slice(c * width, (c + 1) * width)
-        for step in (1, 2, 3):
-            row_copies[c][step].wait_recv()
-        hard_logits = hard_logits + dot_nt(table[0:span, cols], q_v[:, cols])
+    hard_logits = hard_logits + hard_part(CHUNKS - 1)
 
     used = present > 0
     masked = jnp.where(used, hard_logits, -jnp.inf)
@@ -182,20 +225,19 @@
     weights[:, 0:span] = (hard_exp * scale).T.astype(jnp.bfloat16)
     weights[:, span:span + cycle] = (cycle_exp * scale - onehot).T.astype(jnp.bfloat16)
 
-    for step in (1, 2, 3):
-        hot_copies[step].wait_send()
+    for peer in peers:
+        hot_copy(grp, peer, peer).wait_send()
         for c in range(CHUNKS):
-            row_copies[c][step].wait_send()
+            row_copy(grp, peer, c, peer).wait_send()
 
 
 def grad_kernel(table, weights, loss, grad, loss_out, grad_v, sems):
-    tiles = sems.shape[0] - 1
-    width = grad_v.shape[1] // tiles
+    tiles, _, width = table.shape
     copies = [pltpu.make_async_copy(loss, loss_out, sems.at[tiles])]
     copies[0].start()
     for c in range(tiles):
         cols = slice(c * width, (c + 1) * width)
-        grad_v[:, cols] = dot_nn(weights[...], table[:, cols]).astype(jnp.bfloat16)
+        grad_v[:, cols] = dot_nn(weights[...], table[c]).astype(jnp.bfloat16)
         here = pl.ds(c * width, width)
         copies.append(pltpu.make_async_copy(grad_v.at[:, here], grad.at[:, here], sems.at[c]))
         copies[-1].start()
@@ -210,6 +252,7 @@
     _, owners, slots = request_lists.shape
     hn = hard_refs.shape[1]
     span, cycle = owners * slots, n_blk * p_dev
+    width = depth // CHUNKS
     bf16, f32, i32 = jnp.bfloat16, jnp.float32, jnp.int32
     dma = pltpu.SemaphoreType.DMA
     flops = 2 * depth * (2 * q_rows * (span + cycle) + span * pool_rows)
@@ -218,7 +261,7 @@
     table, weights, loss = pl.pallas_call(
         functools.partial(kernel, n_blk),
         out_shape=(
-            pltpu.VMEM((span + cycle, depth), bf16),
+            pltpu.VMEM((CHUNKS, span + cycle, width), bf16),
             pltpu.VMEM((q_rows, span + cycle), bf16),
             pltpu.VMEM((1, q_rows), f32),
         ),
@@ -234,10 +277,10 @@
             pltpu.VMEM((1, q_rows), i32),
             pltpu.VMEM((span, pool_rows), bf16),
             pltpu.VMEM((span, pool_rows), bf16),
-            pltpu.VMEM((span, depth), bf16),
+            pltpu.VMEM((CHUNKS, span, width), bf16),
             pltpu.VMEM((n_blk * TILE_ROWS, depth * p_dev // TILE_ROWS), bf16),
-            dma((7,)), dma((4,)), dma((4,)), dma((4, CHUNKS)), dma((4, CHUNKS)),
-            dma((n_blk,)), dma((n_blk,)),
+            dma((7,)), dma((owners,)), dma((owners,)), dma((owners, CHUNKS)), dma((owners, CHUNKS)),
+            dma((n_blk,)), dma((n_blk,)), pltpu.SemaphoreType.REGULAR,
         ],
         compiler_params=pltpu.CompilerParams(
             collective_id=0, has_side_effects=True, vmem_limit_bytes=VMEM_LIMIT),
@@ -251,7 +294,7 @@
         out_shape=(pltpu.HBM((q_rows, depth), bf16), pltpu.HBM((1, q_rows), f32)),
         in_specs=[in_vmem] * 3,
         out_specs=(in_hbm,) * 2,
-        scratch_shapes=[pltpu.VMEM((q_rows, depth), bf16), dma((GRAD_TILES + 1,))],
+        scratch_shapes=[pltpu.VMEM((q_rows, depth), bf16), dma((CHUNKS + 1,))],
         compiler_params=pltpu.CompilerParams(vmem_limit_bytes=VMEM_LIMIT),
         cost_estimate=pl.CostEstimate(
             flops=2 * depth * q_rows * (span + cycle), bytes_accessed=2 * q_rows * depth, transcendentals=0),

time: 24.9 us -> 22.1 us (0.89)
  Pallas kernels: 24 us -> 21.2 us
    pallas_call x1, Pallas kernels: 22.8 us -> 20 us  [body(): pl.pallas_call(functools.partial(kernel, n_blk), out_shape=(pltpu.VMEM((C...]
where the time goes in v2:
time: 22.1 us; the launch traced here: 21.9 us
  Pallas kernels  21.2 us (96%)
  between operations  0.64 us (3%)
    pallas_call x1, Pallas kernels, body(): pl.pallas_call(functools.partial(kernel, n_blk), out_shape=(pltpu.VMEM((C...  20 us
    pallas_call x1, Pallas kernels, body(): pl.pallas_call(grad_kernel, out_shape=(pltpu.HBM((q_rows, depth), bf16),...  1.23 us

profile of v2, /device:TPU:0, one launch (start us, length us, event | category | flops | bytes accessed | tf_op | source)
XLA Modules:
  0.0 21.9 jit_solution(6314797341750109760)
XLA Ops:
  0.6 20.0 %shard_map.86 = (bf16[4,144,1024]{2,1,0:T(8,128)(2,1)S(1)}, bf16[128,144]{1,0:T(8,128)(2,1)S(1)}, f32[1,128]{1,0:T(1,128)S(1)}) custom-call(bf16[128,4096]{1,0:T(8,128)(2,1)} %queries.1, bf16[2,4096]{1,0:T(2,128)(2,1)} %passages.1, bf16[128,4096]{1,0:T(8,128)(2,1)} %pool.1, s32[1,128]{1,0:T(1,128)} %bitcast.7, s32[4,32]{1,0:T(4,128)} %bitcast.6, ...), custom_call_target="tpu_custom_call" | custom-call | flops 436207616 | bytes 2097152 | tf_op jit(solution)/shard_map/pallas_call | solution.py:261
  20.7 1.2 %shard_map.87 = (bf16[128,4096]{1,0:T(8,128)(2,1)}, f32[1,128]{1,0:T(1,128)}) custom-call(bf16[4,144,1024]{2,1,0:T(8,128)(2,1)S(1)} %get-tuple-element.7.table, bf16[128,144]{1,0:T(8,128)(2,1)S(1)} %get-tuple-element.8.weights, f32[1,128]{1,0:T(1,128)S(1)} %get-tuple-element.9.loss), custom_call_target="tpu_custom_call" | custom-call | flops 150994944 | bytes 1048576 | tf_op jit(solution)/shard_map/pallas_call | solution.py:292

commit v3 on v2

--- a/solution.py
+++ b/solution.py
@@ -110,32 +110,6 @@
 
         lax.fori_loop(1, n_blk, greet, 0)
 
-    hot_in[slot_rows(grp), :] = hot_out[slot_rows(grp), :]
-
-    def send_rows(c, first, last):
-        rows = dot_nn(hot_in[first * slots:last * slots, :], pool_v[:, c * width:(c + 1) * width])
-        picked[c, first * slots:last * slots, :] = rows.astype(jnp.bfloat16)
-        for peer in reversed(range(first, last)):
-            @pl.when(grp != peer)
-            def _():
-                row_copy(grp, peer, c, peer).start()
-
-    def hot_arrived(peer):
-        @pl.when(jnp.logical_and(jnp.logical_not(is_hub), grp != peer))
-        def _():
-            hot_copy(peer, grp, peer).wait_recv()
-
-    loads[2].wait()
-    for peer in range(1, owners):
-        hot_arrived(peer)
-    send_rows(0, 1, owners)
-    send_rows(1, 1, owners)
-    hot_arrived(0)
-    for c in range(CHUNKS):
-        send_rows(c, 0, 1)
-        if c + 2 < CHUNKS:
-            send_rows(c + 2, 1, owners)
-
     loads[1].wait()
     own = pass_v[...].astype(jnp.float32)
     fold_iota = iota((TILE_ROWS, fold_w), 0)
@@ -145,6 +119,38 @@
             folded = jnp.where(fold_iota == c * p_dev + j, own[j:j + 1, c * fold_w:(c + 1) * fold_w], folded)
     own_slot = pl.ds(pl.multiple_of(blk * TILE_ROWS, TILE_ROWS), TILE_ROWS)
     packed[own_slot, :] = folded.astype(jnp.bfloat16)
+
+    hot_in[slot_rows(grp), :] = hot_out[slot_rows(grp), :]
+
+    def pick_rows(c, first, last):
+        rows = dot_nn(hot_in[first * slots:last * slots, :], pool_v[:, c * width:(c + 1) * width])
+        picked[c, first * slots:last * slots, :] = rows.astype(jnp.bfloat16)
+        for peer in range(first, last):
+            @pl.when(half != peer // 2)
+            def _():
+                row_copy(grp, peer, c, peer).start()
+
+    def hot_arrived(peer):
+        @pl.when(jnp.logical_and(jnp.logical_not(is_hub), grp != peer))
+        def _():
+            hot_copy(peer, grp, peer).wait_recv()
+
+    loads[2].wait()
+    for peer in range(1, owners):
+        hot_arrived(peer)
+    pick_rows(0, 1, owners)
+    hot_arrived(0)
+    pick_rows(0, 0, 1)
+    ahead = CHUNKS // 2
+    for c in range(1, CHUNKS):
+        if c < ahead:
+            pick_rows(c, 1, owners)
+            pick_rows(c, 0, 1)
+        else:
+            pick_rows(c, 0, 1)
+            pick_rows(c, 1, owners)
+    for c in range(CHUNKS):
+        row_copy(grp, near, c, near).start()
 
     @pl.when(is_hub)
     def _():

time: 22.1 us -> 22.4 us (1.014)
  Pallas kernels: 21.2 us -> 21.5 us
    pallas_call x1, Pallas kernels: 20 us -> 20.3 us  [body(): pl.pallas_call(functools.partial(kernel, n_blk), out_shape=(pltpu.VMEM((C...]
where the time goes in v3:
time: 22.4 us; the launch traced here: 22.1 us
  Pallas kernels  21.5 us (96%)
  between operations  0.64 us (3%)
    pallas_call x1, Pallas kernels, body(): pl.pallas_call(functools.partial(kernel, n_blk), out_shape=(pltpu.VMEM((C...  20.3 us
    pallas_call x1, Pallas kernels, body(): pl.pallas_call(grad_kernel, out_shape=(pltpu.HBM((q_rows, depth), bf16),...  1.23 us

profile of v3, /device:TPU:0, one launch (start us, length us, event | category | flops | bytes accessed | tf_op | source)
XLA Modules:
  0.0 22.1 jit_solution(15989005824979761223)
XLA Ops:
  0.6 20.3 %shard_map.86 = (bf16[4,144,1024]{2,1,0:T(8,128)(2,1)S(1)}, bf16[128,144]{1,0:T(8,128)(2,1)S(1)}, f32[1,128]{1,0:T(1,128)S(1)}) custom-call(bf16[128,4096]{1,0:T(8,128)(2,1)} %queries.1, bf16[2,4096]{1,0:T(2,128)(2,1)} %passages.1, bf16[128,4096]{1,0:T(8,128)(2,1)} %pool.1, s32[1,128]{1,0:T(1,128)} %bitcast.7, s32[4,32]{1,0:T(4,128)} %bitcast.6, ...), custom_call_target="tpu_custom_call" | custom-call | flops 436207616 | bytes 2097152 | tf_op jit(solution)/shard_map/pallas_call | solution.py:267
  20.9 1.2 %shard_map.87 = (bf16[128,4096]{1,0:T(8,128)(2,1)}, f32[1,128]{1,0:T(1,128)}) custom-call(bf16[4,144,1024]{2,1,0:T(8,128)(2,1)S(1)} %get-tuple-element.7.table, bf16[128,144]{1,0:T(8,128)(2,1)S(1)} %get-tuple-element.8.weights, f32[1,128]{1,0:T(1,128)S(1)} %get-tuple-element.9.loss), custom_call_target="tpu_custom_call" | custom-call | flops 150994944 | bytes 1048576 | tf_op jit(solution)/shard_map/pallas_call | solution.py:298

commit v4 on v3

--- a/solution.py
+++ b/solution.py
@@ -138,17 +138,11 @@
     loads[2].wait()
     for peer in range(1, owners):
         hot_arrived(peer)
-    pick_rows(0, 1, owners)
+    for c in range(CHUNKS):
+        pick_rows(c, 1, owners)
     hot_arrived(0)
-    pick_rows(0, 0, 1)
-    ahead = CHUNKS // 2
-    for c in range(1, CHUNKS):
-        if c < ahead:
-            pick_rows(c, 1, owners)
-            pick_rows(c, 0, 1)
-        else:
-            pick_rows(c, 0, 1)
-            pick_rows(c, 1, owners)
+    for c in range(CHUNKS):
+        pick_rows(c, 0, 1)
     for c in range(CHUNKS):
         row_copy(grp, near, c, near).start()
 

time: 22.4 us -> 21.5 us (0.960)
  Pallas kernels: 21.5 us -> 20.7 us
    pallas_call x1, Pallas kernels: 20.3 us -> 19.5 us  [body(): pl.pallas_call(functools.partial(kernel, n_blk), out_shape=(pltpu.VMEM((C...]
where the time goes in v4:
time: 21.5 us; the launch traced here: 21.3 us
  Pallas kernels  20.7 us (96%)
  between operations  0.64 us (3%)
    pallas_call x1, Pallas kernels, body(): pl.pallas_call(functools.partial(kernel, n_blk), out_shape=(pltpu.VMEM((C...  19.5 us
    pallas_call x1, Pallas kernels, body(): pl.pallas_call(grad_kernel, out_shape=(pltpu.HBM((q_rows, depth), bf16),...  1.23 us

profile of v4, /device:TPU:0, one launch (start us, length us, event | category | flops | bytes accessed | tf_op | source)
XLA Modules:
  0.0 21.3 jit_solution(16722842060067157141)
XLA Ops:
  0.6 19.5 %shard_map.86 = (bf16[4,144,1024]{2,1,0:T(8,128)(2,1)S(1)}, bf16[128,144]{1,0:T(8,128)(2,1)S(1)}, f32[1,128]{1,0:T(1,128)S(1)}) custom-call(bf16[128,4096]{1,0:T(8,128)(2,1)} %queries.1, bf16[2,4096]{1,0:T(2,128)(2,1)} %passages.1, bf16[128,4096]{1,0:T(8,128)(2,1)} %pool.1, s32[1,128]{1,0:T(1,128)} %bitcast.7, s32[4,32]{1,0:T(4,128)} %bitcast.6, ...), custom_call_target="tpu_custom_call" | custom-call | flops 436207616 | bytes 2097152 | tf_op jit(solution)/shard_map/pallas_call | solution.py:261
  20.1 1.2 %shard_map.87 = (bf16[128,4096]{1,0:T(8,128)(2,1)}, f32[1,128]{1,0:T(1,128)}) custom-call(bf16[4,144,1024]{2,1,0:T(8,128)(2,1)S(1)} %get-tuple-element.7.table, bf16[128,144]{1,0:T(8,128)(2,1)S(1)} %get-tuple-element.8.weights, f32[1,128]{1,0:T(1,128)S(1)} %get-tuple-element.9.loss), custom_call_target="tpu_custom_call" | custom-call | flops 150994944 | bytes 1048576 | tf_op jit(solution)/shard_map/pallas_call | solution.py:292

commit v5 on v4

--- a/solution.py
+++ b/solution.py
@@ -138,29 +138,45 @@
     loads[2].wait()
     for peer in range(1, owners):
         hot_arrived(peer)
-    for c in range(CHUNKS):
+    ahead = min(2, CHUNKS)
+
+    def far_sent(c, first, last):
+        for peer in range(first, last):
+            @pl.when(half != peer // 2)
+            def _():
+                row_copy(grp, peer, c, peer).wait_send()
+
+    def send_passes():
+        def send(step, carry):
+            pass_copy(step).start()
+            return carry
+
+        lax.fori_loop(1, n_blk, send, 0)
+
+    for c in range(ahead):
         pick_rows(c, 1, owners)
     hot_arrived(0)
-    for c in range(CHUNKS):
+    for c in range(ahead):
+        pick_rows(c, 0, 1)
+
+    @pl.when(is_hub)
+    def _():
+        pl.semaphore_wait(barrier, n_blk - 1)
+        for peer in peers:
+            pl.semaphore_signal(go_sem, inc=1, device_id={"grp": peer}, device_id_type=MESH)
+
+    @pl.when(jnp.logical_not(is_hub))
+    def _():
+        pl.semaphore_wait(go_sem, 1)
+
+    send_passes()
+    for c in range(ahead, CHUNKS):
+        far_sent(c - ahead, 1, owners)
+        pick_rows(c, 1, owners)
+        far_sent(c - ahead, 0, 1)
         pick_rows(c, 0, 1)
     for c in range(CHUNKS):
         row_copy(grp, near, c, near).start()
-
-    @pl.when(is_hub)
-    def _():
-        pl.semaphore_wait(barrier, n_blk - 1)
-        for peer in peers:
-            pl.semaphore_signal(go_sem, inc=1, device_id={"grp": peer}, device_id_type=MESH)
-
-    @pl.when(jnp.logical_not(is_hub))
-    def _():
-        pl.semaphore_wait(go_sem, 1)
-
-    def send_pass(step, carry):
-        pass_copy(step).start()
-        return carry
-
-    lax.fori_loop(1, n_blk, send_pass, 0)
 
     table[:, slot_rows(grp), :] = picked[:, slot_rows(grp), :]
 
@@ -227,8 +243,10 @@
 
     for peer in peers:
         hot_copy(grp, peer, peer).wait_send()
-        for c in range(CHUNKS):
-            row_copy(grp, peer, c, peer).wait_send()
+    for c in range(CHUNKS):
+        row_copy(grp, near, c, near).wait_send()
+    for c in range(CHUNKS - ahead, CHUNKS):
+        far_sent(c, 0, owners)
 
 
 def grad_kernel(table, weights, loss, grad, loss_out, grad_v, sems):

time: 21.5 us -> 21.9 us (1.019)
  Pallas kernels: 20.7 us -> 21.1 us
    pallas_call x1, Pallas kernels: 19.5 us -> 19.9 us  [body(): pl.pallas_call(functools.partial(kernel, n_blk), out_shape=(pltpu.VMEM((C...]
where the time goes in v5:
time: 21.9 us; the launch traced here: 21.7 us
  Pallas kernels  21.1 us (96%)
  between operations  0.64 us (3%)
    pallas_call x1, Pallas kernels, body(): pl.pallas_call(functools.partial(kernel, n_blk), out_shape=(pltpu.VMEM((C...  19.9 us
    pallas_call x1, Pallas kernels, body(): pl.pallas_call(grad_kernel, out_shape=(pltpu.HBM((q_rows, depth), bf16),...  1.23 us

profile of v5, /device:TPU:0, one launch (start us, length us, event | category | flops | bytes accessed | tf_op | source)
XLA Modules:
  0.0 21.7 jit_solution(7494786846037098318)
XLA Ops:
  0.6 19.9 %shard_map.86 = (bf16[4,144,1024]{2,1,0:T(8,128)(2,1)S(1)}, bf16[128,144]{1,0:T(8,128)(2,1)S(1)}, f32[1,128]{1,0:T(1,128)S(1)}) custom-call(bf16[128,4096]{1,0:T(8,128)(2,1)} %queries.1, bf16[2,4096]{1,0:T(2,128)(2,1)} %passages.1, bf16[128,4096]{1,0:T(8,128)(2,1)} %pool.1, s32[1,128]{1,0:T(1,128)} %bitcast.7, s32[4,32]{1,0:T(4,128)} %bitcast.6, ...), custom_call_target="tpu_custom_call" | custom-call | flops 436207616 | bytes 2097152 | tf_op jit(solution)/shard_map/pallas_call | solution.py:279
  20.5 1.2 %shard_map.87 = (bf16[128,4096]{1,0:T(8,128)(2,1)}, f32[1,128]{1,0:T(1,128)}) custom-call(bf16[4,144,1024]{2,1,0:T(8,128)(2,1)S(1)} %get-tuple-element.7.table, bf16[128,144]{1,0:T(8,128)(2,1)S(1)} %get-tuple-element.8.weights, f32[1,128]{1,0:T(1,128)S(1)} %get-tuple-element.9.loss), custom_call_target="tpu_custom_call" | custom-call | flops 150994944 | bytes 1048576 | tf_op jit(solution)/shard_map/pallas_call | solution.py:310

commit v6 on v4

--- a/solution.py
+++ b/solution.py
@@ -10,7 +10,8 @@
 MESH = pl.DeviceIdType.MESH
 VMEM_LIMIT = 32 * 2**20
 TILE_ROWS = 16
-CHUNKS = 4
+TILES = 8
+CHUNKS = ((0, 1), (1, 2), (3, 2), (5, 2), (7, 1))
 
 
 def iota(shape, axis):
@@ -39,7 +40,7 @@
     cycle = n_blk * p_dev
     folds = TILE_ROWS // p_dev
     fold_w = depth // folds
-    width = depth // CHUNKS
+    width = depth // TILES
 
     half, core = lax.div(grp, 2), lax.rem(grp, 2)
     near, far_odd, far_even = half * 2 + 1 - core, (1 - half) * 2 + 1, (1 - half) * 2
@@ -80,7 +81,8 @@
 
     def row_copy(source, target, c, peer):
         return pltpu.make_async_remote_copy(
-            src_ref=picked.at[c, slot_rows(target)], dst_ref=table.at[c, slot_rows(source)],
+            src_ref=picked.at[pl.ds(*CHUNKS[c]), slot_rows(target)],
+            dst_ref=table.at[pl.ds(*CHUNKS[c]), slot_rows(source)],
             send_sem=row_send.at[target, c], recv_sem=row_recv.at[source, c],
             device_id={"grp": peer}, device_id_type=MESH)
 
@@ -123,8 +125,11 @@
     hot_in[slot_rows(grp), :] = hot_out[slot_rows(grp), :]
 
     def pick_rows(c, first, last):
-        rows = dot_nn(hot_in[first * slots:last * slots, :], pool_v[:, c * width:(c + 1) * width])
-        picked[c, first * slots:last * slots, :] = rows.astype(jnp.bfloat16)
+        tile, count = CHUNKS[c]
+        cols = slice(tile * width, (tile + count) * width)
+        rows = dot_nn(hot_in[first * slots:last * slots, :], pool_v[:, cols]).astype(jnp.bfloat16)
+        for t in range(count):
+            picked[tile + t, first * slots:last * slots, :] = rows[:, t * width:(t + 1) * width]
         for peer in range(first, last):
             @pl.when(half != peer // 2)
             def _():
@@ -138,12 +143,12 @@
     loads[2].wait()
     for peer in range(1, owners):
         hot_arrived(peer)
-    for c in range(CHUNKS):
+    for c in range(len(CHUNKS)):
         pick_rows(c, 1, owners)
     hot_arrived(0)
-    for c in range(CHUNKS):
+    for c in range(len(CHUNKS)):
         pick_rows(c, 0, 1)
-    for c in range(CHUNKS):
+    for c in range(len(CHUNKS)):
         row_copy(grp, near, c, near).start()
 
     @pl.when(is_hub)
@@ -174,13 +179,15 @@
         present = present + (row_iota == refs_t[i:i + 1, :]).astype(jnp.float32)
 
     def hard_part(c):
-        cols = slice(c * width, (c + 1) * width)
         for peer in peers:
             row_copy(peer, grp, c, peer).wait_recv()
-        return dot_nt(table[c, 0:span, :], q_v[:, cols])
+        tile, count = CHUNKS[c]
+        return sum(
+            dot_nt(table[t, 0:span, :], q_v[:, t * width:(t + 1) * width])
+            for t in range(tile, tile + count))
 
     hard_logits = hard_part(0)
-    for c in range(1, CHUNKS - 1):
+    for c in range(1, len(CHUNKS) - 1):
         hard_logits = hard_logits + hard_part(c)
 
     def recv_pass(step, carry):
@@ -205,14 +212,14 @@
 
     lax.fori_loop(0, n_blk // folds, unfold_group, 0)
     cycle_logits = jnp.zeros((cycle, q_rows), jnp.float32)
-    for c in range(CHUNKS):
+    for c in range(TILES):
         cols = slice(c * width, (c + 1) * width)
         cycle_logits = cycle_logits + dot_nt(table[c, span:span + cycle, :], q_v[:, cols])
     cycle_peak = jnp.max(cycle_logits, axis=0, keepdims=True)
     onehot = (iota((cycle, q_rows), 0) == pos_v[...]).astype(jnp.float32)
     chosen = jnp.sum(cycle_logits * onehot, axis=0, keepdims=True)
 
-    hard_logits = hard_logits + hard_part(CHUNKS - 1)
+    hard_logits = hard_logits + hard_part(len(CHUNKS) - 1)
 
     used = present > 0
     masked = jnp.where(used, hard_logits, -jnp.inf)
@@ -227,7 +234,7 @@
 
     for peer in peers:
         hot_copy(grp, peer, peer).wait_send()
-        for c in range(CHUNKS):
+        for c in range(len(CHUNKS)):
             row_copy(grp, peer, c, peer).wait_send()
 
 
@@ -252,7 +259,7 @@
     _, owners, slots = request_lists.shape
     hn = hard_refs.shape[1]
     span, cycle = owners * slots, n_blk * p_dev
-    width = depth // CHUNKS
+    width = depth // TILES
     bf16, f32, i32 = jnp.bfloat16, jnp.float32, jnp.int32
     dma = pltpu.SemaphoreType.DMA
     flops = 2 * depth * (2 * q_rows * (span + cycle) + span * pool_rows)
@@ -261,7 +268,7 @@
     table, weights, loss = pl.pallas_call(
         functools.partial(kernel, n_blk),
         out_shape=(
-            pltpu.VMEM((CHUNKS, span + cycle, width), bf16),
+            pltpu.VMEM((TILES, span + cycle, width), bf16),
             pltpu.VMEM((q_rows, span + cycle), bf16),
             pltpu.VMEM((1, q_rows), f32),
         ),
@@ -277,9 +284,9 @@
             pltpu.VMEM((1, q_rows), i32),
             pltpu.VMEM((span, pool_rows), bf16),
             pltpu.VMEM((span, pool_rows), bf16),
-            pltpu.VMEM((CHUNKS, span, width), bf16),
+            pltpu.VMEM((TILES, span, width), bf16),
             pltpu.VMEM((n_blk * TILE_ROWS, depth * p_dev // TILE_ROWS), bf16),
-            dma((7,)), dma((owners,)), dma((owners,)), dma((owners, CHUNKS)), dma((owners, CHUNKS)),
+            dma((7,)), dma((owners,)), dma((owners,)), dma((owners, len(CHUNKS))), dma((owners, len(CHUNKS))),
             dma((n_blk,)), dma((n_blk,)), pltpu.SemaphoreType.REGULAR,
         ],
         compiler_params=pltpu.CompilerParams(
@@ -294,7 +301,7 @@
         out_shape=(pltpu.HBM((q_rows, depth), bf16), pltpu.HBM((1, q_rows), f32)),
         in_specs=[in_vmem] * 3,
         out_specs=(in_hbm,) * 2,
-        scratch_shapes=[pltpu.VMEM((q_rows, depth), bf16), dma((CHUNKS + 1,))],
+        scratch_shapes=[pltpu.VMEM((q_rows, depth), bf16), dma((TILES + 1,))],
         compiler_params=pltpu.CompilerParams(vmem_limit_bytes=VMEM_LIMIT),
         cost_estimate=pl.CostEstimate(
             flops=2 * depth * q_rows * (span + cycle), bytes_accessed=2 * q_rows * depth, transcendentals=0),

time: 21.5 us -> 21.8 us (1.014)
  Pallas kernels: 20.7 us -> 21 us
    pallas_call x1, Pallas kernels: 19.5 us -> 19.8 us  [body(): pl.pallas_call(functools.partial(kernel, n_blk), out_shape=(pltpu.VMEM((T...]
where the time goes in v6:
time: 21.8 us; the launch traced here: 21.6 us
  Pallas kernels  21 us (96%)
  between operations  0.64 us (3%)
    pallas_call x1, Pallas kernels, body(): pl.pallas_call(functools.partial(kernel, n_blk), out_shape=(pltpu.VMEM((T...  19.8 us
    pallas_call x1, Pallas kernels, body(): pl.pallas_call(grad_kernel, out_shape=(pltpu.HBM((q_rows, depth), bf16),...  1.22 us

profile of v6, /device:TPU:0, one launch (start us, length us, event | category | flops | bytes accessed | tf_op | source)
XLA Modules:
  0.0 21.6 jit_solution(3171152360730617531)
XLA Ops:
  0.6 19.8 %shard_map.86 = (bf16[8,144,512]{2,1,0:T(8,128)(2,1)S(1)}, bf16[128,144]{1,0:T(8,128)(2,1)S(1)}, f32[1,128]{1,0:T(1,128)S(1)}) custom-call(bf16[128,4096]{1,0:T(8,128)(2,1)} %queries.1, bf16[2,4096]{1,0:T(2,128)(2,1)} %passages.1, bf16[128,4096]{1,0:T(8,128)(2,1)} %pool.1, s32[1,128]{1,0:T(1,128)} %bitcast.7, s32[4,32]{1,0:T(4,128)} %bitcast.6, ...), custom_call_target="tpu_custom_call" | custom-call | flops 436207616 | bytes 2097152 | tf_op jit(solution)/shard_map/pallas_call | solution.py:268
  20.4 1.2 %shard_map.87 = (bf16[128,4096]{1,0:T(8,128)(2,1)}, f32[1,128]{1,0:T(1,128)}) custom-call(bf16[8,144,512]{2,1,0:T(8,128)(2,1)S(1)} %get-tuple-element.7.table, bf16[128,144]{1,0:T(8,128)(2,1)S(1)} %get-tuple-element.8.weights, f32[1,128]{1,0:T(1,128)S(1)} %get-tuple-element.9.loss), custom_call_target="tpu_custom_call" | custom-call | flops 150994944 | bytes 1048576 | tf_op jit(solution)/shard_map/pallas_call | solution.py:299

commit v7 on v6

--- a/solution.py
+++ b/solution.py
@@ -10,8 +10,8 @@
 MESH = pl.DeviceIdType.MESH
 VMEM_LIMIT = 32 * 2**20
 TILE_ROWS = 16
-TILES = 8
-CHUNKS = ((0, 1), (1, 2), (3, 2), (5, 2), (7, 1))
+TILES = 4
+CHUNKS = ((0, 1), (1, 2), (3, 1))
 
 
 def iota(shape, axis):

time: 21.8 us -> 21.7 us (level)
  no operation moved by 1% of the time
where the time goes in v7:
time: 21.7 us; the launch traced here: 21.5 us
  Pallas kernels  20.9 us (96%)
  between operations  0.64 us (3%)
    pallas_call x1, Pallas kernels, body(): pl.pallas_call(functools.partial(kernel, n_blk), out_shape=(pltpu.VMEM((T...  19.6 us
    pallas_call x1, Pallas kernels, body(): pl.pallas_call(grad_kernel, out_shape=(pltpu.HBM((q_rows, depth), bf16),...  1.22 us

profile of v7, /device:TPU:0, one launch (start us, length us, event | category | flops | bytes accessed | tf_op | source)
XLA Modules:
  0.0 21.5 jit_solution(16734668231708393082)
XLA Ops:
  0.6 19.6 %shard_map.86 = (bf16[4,144,1024]{2,1,0:T(8,128)(2,1)S(1)}, bf16[128,144]{1,0:T(8,128)(2,1)S(1)}, f32[1,128]{1,0:T(1,128)S(1)}) custom-call(bf16[128,4096]{1,0:T(8,128)(2,1)} %queries.1, bf16[2,4096]{1,0:T(2,128)(2,1)} %passages.1, bf16[128,4096]{1,0:T(8,128)(2,1)} %pool.1, s32[1,128]{1,0:T(1,128)} %bitcast.7, s32[4,32]{1,0:T(4,128)} %bitcast.6, ...), custom_call_target="tpu_custom_call" | custom-call | flops 436207616 | bytes 2097152 | tf_op jit(solution)/shard_map/pallas_call | solution.py:268
  20.3 1.2 %shard_map.87 = (bf16[128,4096]{1,0:T(8,128)(2,1)}, f32[1,128]{1,0:T(1,128)}) custom-call(bf16[4,144,1024]{2,1,0:T(8,128)(2,1)S(1)} %get-tuple-element.7.table, bf16[128,144]{1,0:T(8,128)(2,1)S(1)} %get-tuple-element.8.weights, f32[1,128]{1,0:T(1,128)S(1)} %get-tuple-element.9.loss), custom_call_target="tpu_custom_call" | custom-call | flops 150994944 | bytes 1048576 | tf_op jit(solution)/shard_map/pallas_call | solution.py:299
